TPU v7x, 32 devices: a whole 2x2x4 slice. The times are simulated.
32 devices in a mesh: blk: 8 (over y, x, core), rep: 4 (over z).
Axes of the slice: x: 2, y: 2, z: 4, core: 2. Of those that a mesh axis runs over, the one named last changes fastest.
Arguments:
- generated: float32 [2048, 1024], P(('blk', 'rep')), may hold values from -6 to 6
- real_bank: float32 [16384, 1024], P(('blk', 'rep')), may hold values from -6 to 6
- subset_rows: int32 [8192], P(('blk', 'rep')), may hold values from 0 to 511
Outputs:
- gradient: float32 [2048, 1024], P(('blk', 'rep'))
All inputs are finite; a program needn't handle non-finite values.
Results may differ from a plain program's by a relative error of at most 0.0003.
Values sent between devices are 32-bit elements; how exact they have to be, the bound alone decides.
A program may use at most 128 MiB of HBM per device.

v0:
```python
import jax
import jax.numpy as jnp
from jax import lax
from jax.sharding import PartitionSpec as P

BANDS = (0.5, 1.0, 2.0)


def kernel_weight(dist, width):
    total = jnp.zeros_like(dist)
    for factor in BANDS:
        total = total + jnp.exp(-dist / (2.0 * factor * width)) / factor
    return total


def weight_sums(rows, others):
    row_norms = jnp.sum(rows * rows, axis=1)
    other_norms = jnp.sum(others * others, axis=1)
    inner = jnp.dot(
        rows, others.T, precision=lax.Precision.HIGHEST, preferred_element_type=jnp.float32
    )
    dist = jnp.maximum(row_norms[:, None] + other_norms[None, :] - 2.0 * inner, 0.0)
    weights = kernel_weight(dist, float(rows.shape[1]))
    weighted = jnp.dot(
        weights, others, precision=lax.Precision.HIGHEST, preferred_element_type=jnp.float32
    )
    return (jnp.sum(weights, axis=1), weighted)


def on_device(generated, real_bank, subset_rows):
    total_gen = generated.shape[0] * lax.axis_size("blk") * lax.axis_size("rep")
    total_real = subset_rows.shape[0] * lax.axis_size("blk") * lax.axis_size("rep")
    real_local = jnp.take(real_bank, subset_rows, axis=0)
    gen_block = lax.all_gather(generated, "rep", axis=0, tiled=True)

    def add_pairs(piece):
        sums, weighted = weight_sums(gen_block, piece)
        return (sums, weighted)

    self_total, self_weighted = add_pairs(lax.all_gather(generated, "blk", axis=0, tiled=True))
    cross_total, cross_weighted = add_pairs(lax.all_gather(real_local, "blk", axis=0, tiled=True))
    self_part = self_total[:, None] * gen_block - self_weighted
    cross_part = cross_total[:, None] * gen_block - cross_weighted
    gradient = lax.psum_scatter(
        self_part / total_gen - cross_part / total_real, "rep", scatter_dimension=0, tiled=True
    )
    return gradient


def solution(mesh):
    in_specs = (P(("blk", "rep"), None), P(("blk", "rep"), None), P(("blk", "rep")))
    out_specs = P(("blk", "rep"), None)
    return jax.shard_map(
        on_device, mesh=mesh, in_specs=in_specs, out_specs=out_specs, check_vma=False
    )
```

profile of v0, /device:TPU:0, one launch (start us, length us, event | category | flops | bytes accessed | tf_op | source)
XLA Modules:
  0.0 183.5 jit_solution(10446360388914563249)
XLA Ops:
  6.5 0.0 copy-start
  6.5 0.0 all-gather.4.cloned.1.call-start
  6.5 0.7 all-gather.4.cloned.1.call-update
  7.3 0.0 all-gather.6.cloned.1.call-start
  7.3 0.7 all-gather.6.cloned.1.call-update
  8.0 0.0 all-gather.8.cloned.1.call-start
  8.1 0.7 compare_select_fusion
  8.7 0.0 copy-done
  8.8 0.0 copy-start.6
  8.8 1.1 gather_fusion
  9.8 0.0 copy-done.6
  9.9 1.1 broadcast_select_fusion
  11.0 0.0 all-gather.8.cloned.1.call-update
  11.0 0.0 reduce-scatter.2.cloned.1.call-start
  11.1 28.5 %all-gather.4.cloned.1.call-done = f32[256,1024]{1,0:T(8,128)} async-done(((f32[64,1024]{1,0:T(8,128)}), f32[256,1024]{1,0:T(8,128)}) %all-gather.4.cloned.1.call-update) | async-done | bytes 1048592 | tf_op jit(solution)/shard_map/all_gather | solution.py:34
  39.6 1.5 multiply_reduce_fusion.2
  41.1 27.8 %all-gather.6.cloned.1.call-done = f32[512,1024]{1,0:T(8,128)} async-done(((f32[64,1024]{1,0:T(8,128)}), f32[512,1024]{1,0:T(8,128)}) %all-gather.6.cloned.1.call-update) | async-done | bytes 2097168 | tf_op jit(solution)/shard_map/all_gather | solution.py:40
  68.9 2.0 %multiply_reduce_fusion.1 = f32[512]{0:T(512)S(1)} fusion(f32[512,1024]{1,0:T(8,128)} %all-gather.6.cloned.1.call-done), kind=kLoop, calls=%fused_computation.8 | loop fusion | flops 1048064 | bytes 2099200 | tf_op jit(solution)/shard_map/reduce_sum | solution.py:18
  70.9 0.0 copy-done.4
  70.9 0.3 copy-done.2
  71.1 3.0 %fusion.11 = (f32[256]{0:T(256)S(1)}, f32[256,512]{1,0:T(8,128)}) fusion(f32[256,1024]{1,0:T(8,128)S(1)} %copy-done.4, f32[512,1024]{1,0:T(8,128)S(1)} %copy-done.2, f32[512]{0:T(512)S(1)} %multiply_reduce_fusion.1, f32[256]{0:T(256)S(1)} %multiply_reduce_fusion.2), kind=kOutput, calls=%fused_computation.25 | convolution fusion | flops 1612316416 | bytes 3674112 | tf_op jit(solution)/shard_map/dot_general | solution.py:19
  74.1 51.1 %all-gather.8.cloned.1.call-done = f32[2048,1024]{1,0:T(8,128)} async-done(((f32[256,1024]{1,0:T(8,128)}), f32[2048,1024]{1,0:T(8,128)}) %all-gather.8.cloned.1.call-update) | async-done | bytes 8388624 | tf_op jit(solution)/shard_map/all_gather | solution.py:41
  125.2 4.1 %multiply_reduce_fusion = f32[2048]{0:T(1024)S(1)} fusion(f32[2048,1024]{1,0:T(8,128)} %all-gather.8.cloned.1.call-done), kind=kLoop, calls=%fused_computation.1 | loop fusion | flops 4192256 | bytes 8396800 | tf_op jit(solution)/shard_map/reduce_sum | solution.py:18
  129.4 1.6 copy-done.1
  131.0 8.2 %fusion.10 = (f32[256]{0:T(256)S(1)}, f32[256,2048]{0,1:T(8,128)S(1)}) fusion(f32[2048,1024]{1,0:T(8,128)S(1)} %copy-done.1, f32[256,1024]{1,0:T(8,128)S(1)} %copy-done.4, f32[2048]{0:T(1024)S(1)} %multiply_reduce_fusion, f32[256]{0:T(256)S(1)} %multiply_reduce_fusion.2), kind=kOutput, calls=%fused_computation.24 | convolution fusion | flops 6449266688 | bytes 11544576 | tf_op jit(solution)/shard_map/dot_general | solution.py:19
  139.2 0.0 copy-start.3
  139.2 0.0 copy-start.5
  139.2 7.6 %fusion.6 = f32[256,1024]{1,0:T(8,128)S(1)} fusion(f32[256,2048]{0,1:T(8,128)S(1)} %get-tuple-element.6, f32[2048,1024]{1,0:T(8,128)S(1)} %copy-done.1, f32[256,1024]{1,0:T(8,128)S(1)} %copy-done.4, f32[256]{0:T(256)S(1)} %get-tuple-element.5), kind=kOutput, calls=%fused_computation.13 | convolution fusion | flops 6443237376 | bytes 12583936 | tf_op jit(solution)/shard_map/dot_general | solution.py:24
  146.8 0.0 copy-done.3
  146.8 2.9 %fusion.5 = f32[256,1024]{1,0:T(8,128)} fusion(f32[256,1024]{1,0:T(8,128)S(1)} %fusion.6, f32[256,512]{1,0:T(8,128)S(1)} %copy-done.5, f32[512,1024]{1,0:T(8,128)S(1)} %copy-done.3, f32[256,1024]{1,0:T(8,128)S(1)} %copy-done.4, f32[256]{0:T(256)S(1)} %get-tuple-element.7), kind=kOutput, calls=%fused_computation.11 | convolution fusion | flops 1611661312 | bytes 5768192 | tf_op jit(solution)/shard_map/dot_general | solution.py:24
  149.7 0.0 reduce-scatter.2.cloned.1.call-update
  149.7 27.3 %reduce-scatter.2.cloned.1.call-done = f32[64,1024]{1,0:T(8,128)} async-done(((f32[256,1024]{1,0:T(8,128)}), f32[64,1024]{1,0:T(8,128)}) %reduce-scatter.2.cloned.1.call-update) | async-done | bytes 262160 | tf_op jit(solution)/shard_map/reduce_scatter | solution.py:44
  (6 shorter events, 0.0 us)
Async XLA Ops:
  6.5 2.2 %copy-start = (f32[512,1024]{1,0:T(8,128)S(1)}, f32[512,1024]{1,0:T(8,128)}, u32[]{:S(2)}) copy-start(f32[512,1024]{1,0:T(8,128)} %param.4) | copy-start | bytes 6291460
  6.5 33.1 %all-gather.4.cloned.1.call-start = ((), (), s32[]{:S(2)}) async-start(), calls=%async_computation.1 | async-start | bytes 1310720 | tf_op jit(solution)/shard_map/all_gather | solution.py:34
  7.3 61.6 %all-gather.6.cloned.1.call-start = ((), (), s32[]{:S(2)}) async-start(), calls=%async_computation.2 | async-start | bytes 2359296 | tf_op jit(solution)/shard_map/all_gather | solution.py:40
  8.0 117.2 %all-gather.8.cloned.1.call-start = ((), (), s32[]{:S(2)}) async-start(), calls=%async_computation.3 | async-start | bytes 9437184 | tf_op jit(solution)/shard_map/all_gather | solution.py:41
  8.8 1.1 copy-start.6
  11.0 166.0 %reduce-scatter.2.cloned.1.call-start = ((), (), s32[]{:S(2)}) async-start(), calls=%async_computation.4 | async-start | bytes 1310720 | tf_op jit(solution)/shard_map/reduce_scatter | solution.py:44
  39.6 31.3 %copy-start.4 = (f32[256,1024]{1,0:T(8,128)S(1)}, f32[256,1024]{1,0:T(8,128)}, u32[]{:S(2)}) copy-start(f32[256,1024]{1,0:T(8,128)} %all-gather.4.cloned.1.call-done) | copy-start | bytes 3145732
  68.9 2.2 %copy-start.2 = (f32[512,1024]{1,0:T(8,128)S(1)}, f32[512,1024]{1,0:T(8,128)}, u32[]{:S(2)}) copy-start(f32[512,1024]{1,0:T(8,128)} %all-gather.6.cloned.1.call-done) | copy-start | bytes 6291460
  125.2 5.8 %copy-start.1 = (f32[2048,1024]{1,0:T(8,128)S(1)}, f32[2048,1024]{1,0:T(8,128)}, u32[]{:S(2)}) copy-start(f32[2048,1024]{1,0:T(8,128)} %all-gather.8.cloned.1.call-done) | copy-start | bytes 25165828
  139.2 7.6 %copy-start.3 = (f32[512,1024]{1,0:T(8,128)S(1)}, f32[512,1024]{1,0:T(8,128)}, u32[]{:S(2)}) copy-start(f32[512,1024]{1,0:T(8,128)} %all-gather.6.cloned.1.call-done) | copy-start | bytes 6291460
  139.2 7.6 %copy-start.5 = (f32[256,512]{1,0:T(8,128)S(1)}, f32[256,512]{1,0:T(8,128)}, u32[]{:S(2)}) copy-start(f32[256,512]{1,0:T(8,128)} %get-tuple-element.8) | copy-start | bytes 1572868
Sparse Core Ops, SparseCore 0:
  8.9 30.6 all-gather.3
  41.5 27.3 all-gather.5
  70.8 54.3 all-gather.7
  149.8 27.1 reduce-scatter.1
where the time goes:
time: 184 us
  waiting for transfers between devices  136 us (74%)
  matrix products  21.7 us (12%)
  between operations  13.2 us (7%)
  other arithmetic  9.38 us (5%)
  local copies, waits for them, and re-layouts  2.98 us (2%)
    all_gather x1, waiting for transfers between devices, on_device(): lax.all_gather(real_local, 'blk', axis=0, tiled=True)  51.1 us
    all_gather x1, waiting for transfers between devices, on_device(): gen_block = lax.all_gather(generated, 'rep', axis=0, tiled=True)  28.5 us
    all_gather x1, waiting for transfers between devices, on_device(): lax.all_gather(generated, 'blk', axis=0, tiled=True)  27.8 us
    reduce_scatter x1, waiting for transfers between devices, on_device(): lax.psum_scatter(self_part / total_gen - cross_part / total_real, 'rep',...  27.3 us
    dot_general x2, matrix products, weight_sums(): jnp.dot(rows, others.T, precision=lax.Precision.HIGHEST, preferred_elemen...  11.2 us
    dot_general x2, matrix products, weight_sums(): jnp.dot(weights, others, precision=lax.Precision.HIGHEST, preferred_eleme...  10.5 us
    reduce_sum x2, other arithmetic, weight_sums(): other_norms = jnp.sum(others * others, axis=1)  6.1 us
  transfers between devices with their start and end apart: 4, of which 4 were waited for; matrix products, arithmetic and copies ran while one was open for 5% of the time, Pallas kernels for 0%

commit v1 on v0

v1 whole, which is shorter than its diff:
```python
import functools

import jax
import jax.numpy as jnp
from jax import lax
from jax.experimental import pallas as pl
from jax.experimental.pallas import tpu as pltpu
from jax.sharding import PartitionSpec as P

MESH = pl.DeviceIdType.MESH
GROUP = 4
PIECES = 4


def split(value):
    high = value.astype(jnp.bfloat16)
    return high, (value - high.astype(jnp.float32)).astype(jnp.bfloat16)


def dot(a, b, contract):
    return lax.dot_general(a, b, (contract, ((), ())), preferred_element_type=jnp.float32)


def product(a_high, a_low, b_high, b_low, contract):
    return (
        dot(a_high, b_high, contract)
        + dot(a_high, b_low, contract)
        + dot(a_low, b_high, contract)
    )


def kernel(
    sizes,
    rows_ref, gen_ref, bank_ref, out_ref,
    oth, oth_high, oth_low, oth_norm,
    gen, gen_high, gen_low, gen_norm, acc, total, from_hi, from_z,
    sib_send, sib_recv, far_send, far_recv, fwd_send, fwd_recv,
    z_send, z_recv, hi_send, hi_recv, red_hi_send, red_hi_recv, red_z_send, red_z_recv,
):
    blks, reps = sizes
    his = blks // GROUP
    n_gen, width = gen_ref.shape
    n_real = rows_ref.shape[0]
    piece = n_real // PIECES
    total_gen = n_gen * blks * reps
    total_real = n_real * blks * reps
    group = reps * n_gen

    blk, rep = lax.axis_index("blk"), lax.axis_index("rep")
    hi, lo = blk // GROUP, lax.rem(blk, GROUP)
    core, side = lax.rem(lo, 2), lo // 2
    sibling = (hi * GROUP + side * 2 + (1 - core), rep)
    across = (hi * GROUP + (1 - side) * 2 + core, rep)

    def z_partner(dz):
        return (blk, lax.rem(rep + dz, reps))

    def hi_partner(dh):
        return (lax.rem(hi + dh, his) * GROUP + lo, rep)

    half = n_real // 2
    starts = (0, n_real, 2 * n_real, 2 * n_real + GROUP * n_gen)
    c_gen, c_far = starts[2], starts[3]
    n_chunks = 5

    def far_rows(m, forwarded):
        chunk, part = divmod(m, PIECES // 2)
        return pl.ds(c_far + chunk * n_real + (half if forwarded else 0) + part * piece, piece)

    def gen_rows(slot):
        return pl.ds(c_gen + slot * n_gen, n_gen)

    def block(dh, dz):
        return pl.ds(dh * group + dz * n_gen, n_gen)

    def remote(src, dst, send, recv, device):
        return pltpu.make_async_remote_copy(
            src_ref=src, dst_ref=dst, send_sem=send, recv_sem=recv, device_id=device, device_id_type=MESH
        )

    partners = [sibling, across]
    partners += [z_partner(dz) for dz in range(1, reps)]
    partners += [hi_partner(dh) for dh in range(1, his)]
    barrier = pltpu.get_barrier_semaphore()
    for device in partners:
        pl.semaphore_signal(barrier, inc=1, device_id=device, device_id_type=MESH)

    def gather(i, carry):
        for k in range(8):
            p = i * 8 + k
            oth[pl.ds(p, 1), :] = bank_ref[pl.ds(rows_ref[p], 1), :]
        return carry

    lax.fori_loop(0, piece // 8, gather, 0)
    pl.semaphore_wait(barrier, len(partners))

    sent = []

    def start(copy):
        copy.start()
        sent.append(copy)
        return copy

    far_gen = start(remote(gen_ref, oth.at[gen_rows(2)], far_send.at[0], far_recv.at[0], across))
    z_copies, hi_copies = {}, {}
    z_order = [dz for dz in (2, 1, 3) if dz < reps] + list(range(4, reps))
    for dz in z_order:
        back = reps - dz
        z_copies[back] = start(
            remote(gen_ref, gen.at[block(0, back)], z_send.at[dz], z_recv.at[back], z_partner(dz))
        )
    for dh in range(1, his):
        back = his - dh
        hi_copies[back, 0] = start(
            remote(
                gen_ref, gen.at[block(back, 0)], hi_send.at[dh, 0], hi_recv.at[back, 0], hi_partner(dh)
            )
        )
    sib_gen = start(remote(gen_ref, oth.at[gen_rows(1)], sib_send.at[0], sib_recv.at[0], sibling))

    far_real = []
    for m in range(PIECES):
        if m > 0:
            lax.fori_loop(m * piece // 8, (m + 1) * piece // 8, gather, 0)
        far_real.append(
            start(
                remote(
                    oth.at[pl.ds(m * piece, piece)], oth.at[far_rows(m, False)],
                    far_send.at[1 + m], far_recv.at[1 + m], across,
                )
            )
        )
    sib_real = start(
        remote(oth.at[pl.ds(0, n_real)], oth.at[pl.ds(n_real, n_real)], sib_send.at[1], sib_recv.at[1], sibling)
    )

    def forward(rows, to, index):
        return start(remote(oth.at[rows], oth.at[to], fwd_send.at[index], fwd_recv.at[index], sibling))

    def prepare_other(start_row, count, chunk):
        rows = pl.ds(start_row, count)
        value = oth[rows, :]
        high, low = split(value)
        oth_high[rows, :] = high
        oth_low[rows, :] = low
        ones = jnp.ones((8, width), jnp.float32)
        oth_norm[chunk] = lax.dot_general(
            ones, value * value, (((1,), (1,)), ((), ())),
            precision=lax.Precision.HIGHEST, preferred_element_type=jnp.float32,
        )

    def prepare_gen(rows):
        value = gen[rows, :]
        high, low = split(value)
        gen_high[rows, :] = high
        gen_low[rows, :] = low
        gen_norm[rows, :] = jnp.sum(value * value, axis=1, keepdims=True)

    def add_pairs(row_start, other_start, chunk, scale, first=False):
        rows = pl.ds(row_start, group)
        others = pl.ds(other_start, n_real)
        inner = product(
            gen_high[rows, :], gen_low[rows, :], oth_high[others, :], oth_low[others, :], ((1,), (1,))
        )
        dist = jnp.maximum(gen_norm[rows, :] + oth_norm[chunk, 0:1, :] - 2.0 * inner, 0.0)
        wide = jnp.exp(dist * (-1.0 / (4.0 * width)))
        middle = wide * wide
        weight = (2.0 * (middle * middle) + middle + 0.5 * wide) * scale
        sums = jnp.sum(weight, axis=1, keepdims=True)
        w_high, w_low = split(weight)
        step = 256
        for column in range(0, width, step):
            columns = pl.ds(column, step)
            part = product(w_high, w_low, oth_high[others, columns], oth_low[others, columns], ((1,), (0,)))
            acc[rows, columns] = part if first else acc[rows, columns] + part
        total[rows, :] = sums if first else total[rows, :] + sums

    def finish(row_start):
        rows = pl.ds(row_start, group)
        acc[rows, :] = total[rows, :] * gen[rows, :] - acc[rows, :]

    self_scale, cross_scale = 1.0 / total_gen, -1.0 / total_real

    gen[block(0, 0), :] = gen_ref[...]
    prepare_gen(block(0, 0))
    oth[gen_rows(0), :] = gen_ref[...]
    prepare_other(0, n_real, 0)

    for dz in z_order:
        z_copies[dz].wait_recv()
        for dh in range(1, his):
            back = his - dh
            hi_copies[back, dz] = start(
                remote(
                    gen.at[block(0, dz)], gen.at[block(back, dz)],
                    hi_send.at[dh, dz], hi_recv.at[back, dz], hi_partner(dh),
                )
            )
        prepare_gen(block(0, dz))
    far_gen.wait_recv()
    forwards = [forward(gen_rows(2), gen_rows(3), 0)]

    add_pairs(0, 0, 0, cross_scale, first=True)
    sib_gen.wait_recv()
    sib_real.wait_recv()
    prepare_other(n_real, n_real, 1)
    add_pairs(0, n_real, 1, cross_scale)
    forwards[0].wait_recv()
    prepare_other(c_gen, GROUP * n_gen, 2)
    add_pairs(0, c_gen, 2, self_scale)

    def take_far(m):
        far_real[m].wait_recv()
        forwards.append(forward(far_rows(m, False), far_rows(m, True), 1 + m))

    for m in range(PIECES // 2):
        take_far(m)

    for dh in range(1, his):
        for dz in range(reps):
            hi_copies[dh, dz].wait_recv()

    def later_rows(dh, carry):
        row_start = pl.multiple_of(dh * group, group)
        for dz in range(reps):
            prepare_gen(pl.ds(row_start + dz * n_gen, n_gen))
        add_pairs(row_start, 0, 0, cross_scale, first=True)

        def chunk_pairs(c, inner_carry):
            scale = jnp.where(c == 2, self_scale, cross_scale)
            add_pairs(row_start, pl.multiple_of(c * n_real, n_real), c, scale)
            return inner_carry

        lax.fori_loop(1, 3, chunk_pairs, 0)
        return carry

    lax.fori_loop(1, his, later_rows, 0)

    for m in range(PIECES // 2):
        forwards[1 + m].wait_recv()
    prepare_other(c_far, n_real, 3)

    def third_chunk(dh, carry):
        add_pairs(pl.multiple_of(dh * group, group), c_far, 3, cross_scale)
        return carry

    lax.fori_loop(0, his, third_chunk, 0)

    for m in range(PIECES // 2, PIECES):
        take_far(m)
    for m in range(PIECES // 2, PIECES):
        forwards[1 + m].wait_recv()
    prepare_other(c_far + n_real, n_real, 4)

    red_hi = {}
    for dh in range(1, his):
        back = his - dh
        add_pairs(dh * group, c_far + n_real, 4, cross_scale)
        finish(dh * group)
        for dz in z_order + [0]:
            red_hi[back, dz] = start(
                remote(
                    acc.at[block(dh, dz)], from_hi.at[back, dz],
                    red_hi_send.at[dh, dz], red_hi_recv.at[back, dz], hi_partner(dh),
                )
            )
    add_pairs(0, c_far + n_real, 4, cross_scale)
    finish(0)

    red_z = {}
    for dz in z_order + [0]:
        for dh in range(1, his):
            red_hi[dh, dz].wait_recv()
            acc[block(0, dz), :] = acc[block(0, dz), :] + from_hi[dh, dz]
        if dz > 0:
            back = reps - dz
            red_z[back] = start(
                remote(
                    acc.at[block(0, dz)], from_z.at[back],
                    red_z_send.at[dz], red_z_recv.at[back], z_partner(dz),
                )
            )
    result = acc[block(0, 0), :]
    for dz in z_order:
        red_z[dz].wait_recv()
        result = result + from_z[dz]
    out_ref[...] = result

    for copy in sent:
        copy.wait_send()


def solution(mesh):
    blks, reps = mesh.shape["blk"], mesh.shape["rep"]
    his = blks // GROUP

    def on_device(generated, real_bank, subset_rows):
        n_gen, width = generated.shape
        n_real = subset_rows.shape[0]
        n_other = 5 * n_real
        n_rows = his * reps * n_gen
        dma = pltpu.SemaphoreType.DMA
        vmem = pl.BlockSpec(memory_space=pltpu.VMEM)
        pairs = n_rows * n_other
        return pl.pallas_call(
            functools.partial(kernel, (blks, reps)),
            out_shape=jax.ShapeDtypeStruct((n_gen, width), jnp.float32),
            in_specs=[pl.BlockSpec(memory_space=pltpu.SMEM), vmem, vmem],
            out_specs=vmem,
            scratch_shapes=[
                pltpu.VMEM((n_other, width), jnp.float32),
                pltpu.VMEM((n_other, width), jnp.bfloat16),
                pltpu.VMEM((n_other, width), jnp.bfloat16),
                pltpu.VMEM((5, 8, n_real), jnp.float32),
                pltpu.VMEM((n_rows, width), jnp.float32),
                pltpu.VMEM((n_rows, width), jnp.bfloat16),
                pltpu.VMEM((n_rows, width), jnp.bfloat16),
                pltpu.VMEM((n_rows, 1), jnp.float32),
                pltpu.VMEM((n_rows, width), jnp.float32),
                pltpu.VMEM((n_rows, 1), jnp.float32),
                pltpu.VMEM((his, reps, n_gen, width), jnp.float32),
                pltpu.VMEM((reps, n_gen, width), jnp.float32),
                dma((2,)), dma((2,)),
                dma((1 + PIECES,)), dma((1 + PIECES,)),
                dma((1 + PIECES,)), dma((1 + PIECES,)),
                dma((reps,)), dma((reps,)),
                dma((his, reps)), dma((his, reps)),
                dma((his, reps)), dma((his, reps)),
                dma((reps,)), dma((reps,)),
            ],
            compiler_params=pltpu.CompilerParams(
                collective_id=0, has_side_effects=True, vmem_limit_bytes=60 * 1024 * 1024
            ),
            cost_estimate=pl.CostEstimate(
                flops=12 * pairs * width, bytes_accessed=4 * 1024 * width, transcendentals=pairs
            ),
        )(subset_rows, generated, real_bank)

    in_specs = (P(("blk", "rep"), None), P(("blk", "rep"), None), P(("blk", "rep")))
    return jax.shard_map(
        on_device, mesh=mesh, in_specs=in_specs, out_specs=P(("blk", "rep"), None), check_vma=False
    )
```

time: 184 us -> 89.9 us (0.49)
  the two profiles are of different devices: /device:TPU:0 before, /device:TPU:23 now
where the time goes in v1:
time: 89.9 us; the launch traced here: 89.7 us
  Pallas kernels  88 us (98%)
  local copies, waits for them, and re-layouts  1.67 us (2%)
    pallas_call x1, Pallas kernels, on_device(): pl.pallas_call(functools.partial(kernel, (blks, reps)), out_shape=jax.Sha...  88 us

profile of v1, /device:TPU:23, one launch (start us, length us, event | category | flops | bytes accessed | tf_op | source)
XLA Modules:
  0.0 89.7 jit_solution(3190081280370143440)
XLA Ops:
  0.0 88.0 %shard_map.37 = f32[64,1024]{1,0:T(8,128)} custom-call(s32[256]{0:T(256)} %rows_ref.1, f32[64,1024]{1,0:T(8,128)} %gen_ref.1, f32[512,1024]{1,0:T(8,128)} %bank_ref.1), custom_call_target="tpu_custom_call" | custom-call | flops 8053063680 | bytes 4194304 | tf_op jit(solution)/shard_map/pallas_call | solution.py:305
  88.0 1.7 %copy.5 = f32[64,1024]{1,0:T(8,128)} copy(f32[64,1024]{1,0:T(8,128)} %shard_map.37) | data formatting | bytes 524288

commit v2 on v1

v2 whole, which is shorter than its diff:
```python
import functools

import jax
import jax.numpy as jnp
from jax import lax
from jax.experimental import pallas as pl
from jax.experimental.pallas import tpu as pltpu
from jax.sharding import PartitionSpec as P

MESH = pl.DeviceIdType.MESH
GROUP = 4
PAIR = 2
PIECES = 4


def split(value):
    high = value.astype(jnp.bfloat16)
    return high, (value - high.astype(jnp.float32)).astype(jnp.bfloat16)


def dot(a, b, contract):
    return lax.dot_general(a, b, (contract, ((), ())), preferred_element_type=jnp.float32)


def product(a_high, a_low, b_high, b_low, contract):
    return (
        dot(a_high, b_high, contract)
        + dot(a_high, b_low, contract)
        + dot(a_low, b_high, contract)
    )


def kernel(
    sizes,
    rows_ref, gen_ref, bank_ref, out_ref, bank, bank_sem,
    oth, oth_high, oth_low, oth_norm,
    gen, gen_high, gen_low, gen_norm, acc, total, from_hi, from_z,
    sib_send, sib_recv, far_send, far_recv, fwd_send, fwd_recv,
    z_send, z_recv, hi_send, hi_recv, red_hi_send, red_hi_recv, red_z_send, red_z_recv,
):
    blks, reps = sizes
    his = blks // GROUP
    n_gen, width = gen_ref.shape
    n_real = rows_ref.shape[0]
    piece = n_real // PIECES
    total_gen = n_gen * blks * reps
    total_real = n_real * blks * reps
    tile = PAIR * n_gen
    near_tiles = reps // PAIR
    n_tiles = his * near_tiles

    blk, rep = lax.axis_index("blk"), lax.axis_index("rep")
    hi, lo = blk // GROUP, lax.rem(blk, GROUP)
    core, side = lax.rem(lo, 2), lo // 2
    sibling = (hi * GROUP + side * 2 + (1 - core), rep)
    across = (hi * GROUP + (1 - side) * 2 + core, rep)

    def z_partner(dz):
        return (blk, lax.rem(rep + dz, reps))

    def hi_partner(dh):
        return (lax.rem(hi + dh, his) * GROUP + lo, rep)

    half = n_real // 2
    c_gen, c_far = 2 * n_real, 3 * n_real

    def far_rows(m, forwarded):
        chunk, part = divmod(m, PIECES // 2)
        return pl.ds(c_far + chunk * n_real + (half if forwarded else 0) + part * piece, piece)

    def gen_rows(slot):
        return pl.ds(c_gen + slot * n_gen, n_gen)

    def block(dh, dz):
        return pl.ds(pl.multiple_of((dh * reps + dz) * n_gen, n_gen), n_gen)

    def remote(src, dst, send, recv, device):
        return pltpu.make_async_remote_copy(
            src_ref=src, dst_ref=dst, send_sem=send, recv_sem=recv, device_id=device, device_id_type=MESH
        )

    def z_copy(dz):
        back = reps - dz
        return remote(gen_ref, gen.at[block(0, back)], z_send.at[dz], z_recv.at[back], z_partner(dz))

    def hi_copy(dh, dz, src):
        back = his - dh
        return remote(src, gen.at[block(back, dz)], hi_send.at[dh, dz], hi_recv.at[back, dz], hi_partner(dh))

    def far_gen():
        return remote(gen_ref, oth.at[gen_rows(2)], far_send.at[0], far_recv.at[0], across)

    def far_real(m):
        return remote(
            oth.at[pl.ds(m * piece, piece)], oth.at[far_rows(m, False)],
            far_send.at[1 + m], far_recv.at[1 + m], across,
        )

    def sib_gen():
        return remote(gen_ref, oth.at[gen_rows(1)], sib_send.at[0], sib_recv.at[0], sibling)

    def sib_real():
        return remote(
            oth.at[pl.ds(0, n_real)], oth.at[pl.ds(n_real, n_real)], sib_send.at[1], sib_recv.at[1], sibling
        )

    def forward_gen():
        return remote(oth.at[gen_rows(2)], oth.at[gen_rows(3)], fwd_send.at[0], fwd_recv.at[0], sibling)

    def forward_real(m):
        return remote(
            oth.at[far_rows(m, False)], oth.at[far_rows(m, True)],
            fwd_send.at[1 + m], fwd_recv.at[1 + m], sibling,
        )

    def red_hi(dh, dz):
        back = his - dh
        return remote(
            acc.at[block(dh, dz)], from_hi.at[back, dz],
            red_hi_send.at[dh, dz], red_hi_recv.at[back, dz], hi_partner(dh),
        )

    def red_z(dz):
        back = reps - dz
        return remote(
            acc.at[block(0, dz)], from_z.at[back], red_z_send.at[dz], red_z_recv.at[back], z_partner(dz)
        )

    load_bank = pltpu.make_async_copy(bank_ref, bank, bank_sem)
    load_bank.start()
    partners = [sibling, across]
    partners += [z_partner(dz) for dz in range(1, reps)]
    partners += [hi_partner(dh) for dh in range(1, his)]
    barrier = pltpu.get_barrier_semaphore()
    for device in partners:
        pl.semaphore_signal(barrier, inc=1, device_id=device, device_id_type=MESH)
    load_bank.wait()

    def gather(i, carry):
        for k in range(8):
            p = i * 8 + k
            oth[pl.ds(p, 1), :] = bank[pl.ds(rows_ref[p], 1), :]
        return carry

    lax.fori_loop(0, piece // 8, gather, 0)
    pl.semaphore_wait(barrier, len(partners))

    far_gen().start()
    z_copy(1).start()
    for dh in range(1, his):
        hi_copy(dh, 0, gen_ref).start()
    for dz in range(2, reps):
        z_copy(dz).start()
    sib_gen().start()

    far_real(0).start()
    for m in range(1, PIECES):
        lax.fori_loop(m * piece // 8, (m + 1) * piece // 8, gather, 0)
        far_real(m).start()
    sib_real().start()

    def prepare_other(chunk):
        rows = pl.ds(chunk * n_real, n_real)
        value = oth[rows, :]
        high, low = split(value)
        oth_high[rows, :] = high
        oth_low[rows, :] = low
        norm = jnp.sum(value * value, axis=1, keepdims=True)
        oth_norm[chunk] = jnp.broadcast_to(norm, (n_real, 128)).T[0:8, :]

    def prepare_gen(rows):
        value = gen[rows, :]
        high, low = split(value)
        gen_high[rows, :] = high
        gen_low[rows, :] = low
        gen_norm[rows, :] = jnp.sum(value * value, axis=1, keepdims=True)

    def tile_rows(q):
        return pl.ds(pl.multiple_of(q * tile, tile), tile)

    def add_pairs(q, chunk, scale):
        rows = tile_rows(q)
        others = pl.ds(pl.multiple_of(chunk * n_real, n_real), n_real)
        inner = product(
            gen_high[rows, :], gen_low[rows, :], oth_high[others, :], oth_low[others, :], ((1,), (1,))
        )
        dist = jnp.maximum(gen_norm[rows, :] + oth_norm[chunk, 0:1, :] - 2.0 * inner, 0.0)
        wide = jnp.exp(dist * (-1.0 / (4.0 * width)))
        middle = wide * wide
        weight = (2.0 * (middle * middle) + middle + 0.5 * wide) * scale
        total[rows, :] += jnp.sum(weight, axis=1, keepdims=True)
        w_high, w_low = split(weight)
        step = 256
        for column in range(0, width, step):
            columns = pl.ds(column, step)
            acc[rows, columns] += product(
                w_high, w_low, oth_high[others, columns], oth_low[others, columns], ((1,), (0,))
            )

    self_scale, cross_scale = 1.0 / total_gen, -1.0 / total_real

    def take_far(m):
        far_real(m).wait_recv()
        forward_real(m).start()

    def take_z(dz):
        z_copy(reps - dz).wait_recv()
        for dh in range(1, his):
            hi_copy(dh, dz, gen.at[block(0, dz)]).start()

    gen[block(0, 0), :] = gen_ref[...]
    oth[gen_rows(0), :] = gen_ref[...]
    prepare_other(0)
    far_gen().wait_recv()
    forward_gen().start()
    for dz in range(1, PAIR):
        take_z(dz)
    sib_gen().wait_recv()
    sib_real().wait_recv()
    prepare_other(1)
    forward_gen().wait_recv()
    prepare_other(2)

    def first_chunks(q, carry):
        for k in range(1, near_tiles):

            @pl.when(q == k)
            def _():
                for dz in range(k * PAIR, (k + 1) * PAIR):
                    take_z(dz)

        @pl.when(q == 1)
        def _():
            for m in range(PIECES // 2):
                take_far(m)

        @pl.when(q >= near_tiles)
        def _():
            for i in range(PAIR):
                dh, dz = q // near_tiles, lax.rem(q, near_tiles) * PAIR + i
                hi_copy(his - dh, dz, gen_ref).wait_recv()

        rows = tile_rows(q)
        prepare_gen(rows)
        acc[rows, :] = jnp.zeros((tile, width), jnp.float32)
        total[rows, :] = jnp.zeros((tile, 1), jnp.float32)

        def chunk_pairs(chunk, inner_carry):
            add_pairs(q, chunk, jnp.where(chunk == 2, self_scale, cross_scale))
            return inner_carry

        lax.fori_loop(0, 3, chunk_pairs, 0)
        return carry

    lax.fori_loop(0, n_tiles, first_chunks, 0)

    take_far(PIECES // 2)
    for m in range(PIECES // 2):
        forward_real(m).wait_recv()
    prepare_other(3)

    def third_chunk(q, carry):
        add_pairs(q, 3, cross_scale)
        return carry

    lax.fori_loop(0, n_tiles, third_chunk, 0)

    for m in range(PIECES // 2 + 1, PIECES):
        take_far(m)
    for m in range(PIECES // 2, PIECES):
        forward_real(m).wait_recv()
    prepare_other(4)

    def last_chunk(i, carry):
        q = n_tiles - 1 - i
        add_pairs(q, 4, cross_scale)
        rows = tile_rows(q)
        acc[rows, :] = total[rows, :] * gen[rows, :] - acc[rows, :]

        @pl.when(q >= near_tiles)
        def _():
            for k in reversed(range(PAIR)):
                dh, dz = q // near_tiles, lax.rem(q, near_tiles) * PAIR + k
                red_hi(dh, dz).start()

        return carry

    lax.fori_loop(0, n_tiles, last_chunk, 0)

    for dz in reversed(range(reps)):
        for dh in range(1, his):
            red_hi(his - dh, dz).wait_recv()
            acc[block(0, dz), :] += from_hi[dh, dz]
        if dz > 0:
            red_z(dz).start()
    result = acc[block(0, 0), :]
    for dz in reversed(range(1, reps)):
        red_z(reps - dz).wait_recv()
        result = result + from_z[dz]
    out_ref[...] = result

    sent = [far_gen(), sib_gen(), sib_real(), forward_gen()]
    sent += [far_real(m) for m in range(PIECES)] + [forward_real(m) for m in range(PIECES)]
    sent += [z_copy(dz) for dz in range(1, reps)] + [red_z(dz) for dz in range(1, reps)]
    sent += [hi_copy(dh, dz, gen_ref) for dh in range(1, his) for dz in range(reps)]
    sent += [red_hi(dh, dz) for dh in range(1, his) for dz in range(reps)]
    for copy in sent:
        copy.wait_send()


def solution(mesh):
    blks, reps = mesh.shape["blk"], mesh.shape["rep"]
    his = blks // GROUP

    def on_device(generated, real_bank, subset_rows):
        n_gen, width = generated.shape
        n_real = subset_rows.shape[0]
        n_other = 5 * n_real
        n_rows = his * reps * n_gen
        dma = pltpu.SemaphoreType.DMA
        vmem = pl.BlockSpec(memory_space=pltpu.VMEM)
        pairs = n_rows * n_other
        return pl.pallas_call(
            functools.partial(kernel, (blks, reps)),
            out_shape=jax.ShapeDtypeStruct((n_gen, width), jnp.float32),
            in_specs=[pl.BlockSpec(memory_space=pltpu.SMEM), vmem, pl.BlockSpec(memory_space=pl.ANY)],
            out_specs=vmem,
            scratch_shapes=[
                pltpu.VMEM(real_bank.shape, jnp.float32),
                dma(()),
                pltpu.VMEM((n_other, width), jnp.float32),
                pltpu.VMEM((n_other, width), jnp.bfloat16),
                pltpu.VMEM((n_other, width), jnp.bfloat16),
                pltpu.VMEM((5, 8, n_real), jnp.float32),
                pltpu.VMEM((n_rows, width), jnp.float32),
                pltpu.VMEM((n_rows, width), jnp.bfloat16),
                pltpu.VMEM((n_rows, width), jnp.bfloat16),
                pltpu.VMEM((n_rows, 1), jnp.float32),
                pltpu.VMEM((n_rows, width), jnp.float32),
                pltpu.VMEM((n_rows, 1), jnp.float32),
                pltpu.VMEM((his, reps, n_gen, width), jnp.float32),
                pltpu.VMEM((reps, n_gen, width), jnp.float32),
                dma((2,)), dma((2,)),
                dma((1 + PIECES,)), dma((1 + PIECES,)),
                dma((1 + PIECES,)), dma((1 + PIECES,)),
                dma((reps,)), dma((reps,)),
                dma((his, reps)), dma((his, reps)),
                dma((his, reps)), dma((his, reps)),
                dma((reps,)), dma((reps,)),
            ],
            compiler_params=pltpu.CompilerParams(
                collective_id=0, has_side_effects=True, vmem_limit_bytes=60 * 1024 * 1024
            ),
            cost_estimate=pl.CostEstimate(
                flops=12 * pairs * width, bytes_accessed=4 * 1024 * width, transcendentals=pairs
            ),
        )(subset_rows, generated, real_bank)

    in_specs = (P(("blk", "rep"), None), P(("blk", "rep"), None), P(("blk", "rep")))
    return jax.shard_map(
        on_device, mesh=mesh, in_specs=in_specs, out_specs=P(("blk", "rep"), None), check_vma=False
    )
```

time: 89.9 us -> 91 us (1.012)
  the two profiles are of different devices: /device:TPU:23 before, /device:TPU:0 now
where the time goes in v2:
time: 91 us; the launch traced here: 90.8 us
  Pallas kernels  89.1 us (98%)
  local copies, waits for them, and re-layouts  1.67 us (2%)
    pallas_call x1, Pallas kernels, on_device(): pl.pallas_call(functools.partial(kernel, (blks, reps)), out_shape=jax.Sha...  89.1 us

profile of v2, /device:TPU:0, one launch (start us, length us, event | category | flops | bytes accessed | tf_op | source)
XLA Modules:
  0.0 90.8 jit_solution(10824740800277051395)
XLA Ops:
  0.0 89.1 %shard_map.37 = f32[64,1024]{1,0:T(8,128)} custom-call(s32[256]{0:T(256)} %rows_ref.1, f32[64,1024]{1,0:T(8,128)} %gen_ref.1, f32[512,1024]{1,0:T(8,128)} %bank_ref.1), custom_call_target="tpu_custom_call" | custom-call | flops 8053063680 | bytes 4194304 | tf_op jit(solution)/shard_map/pallas_call | solution.py:323
  89.1 1.7 %copy.5 = f32[64,1024]{1,0:T(8,128)} copy(f32[64,1024]{1,0:T(8,128)} %shard_map.37) | data formatting | bytes 524288

commit v3 on v2

--- a/solution.py
+++ b/solution.py
@@ -9,7 +9,6 @@
 
 MESH = pl.DeviceIdType.MESH
 GROUP = 4
-PAIR = 2
 PIECES = 4
 
 
@@ -22,19 +21,17 @@
     return lax.dot_general(a, b, (contract, ((), ())), preferred_element_type=jnp.float32)
 
 
-def product(a_high, a_low, b_high, b_low, contract):
-    return (
-        dot(a_high, b_high, contract)
-        + dot(a_high, b_low, contract)
-        + dot(a_low, b_high, contract)
-    )
+def product(a_both, a_high, b_high, b_low, contract):
+    rows = a_high.shape[0]
+    both = dot(a_both, b_high, contract)
+    return both[:rows] + (both[rows:] + dot(a_high, b_low, contract))
 
 
 def kernel(
     sizes,
     rows_ref, gen_ref, bank_ref, out_ref, bank, bank_sem,
     oth, oth_high, oth_low, oth_norm,
-    gen, gen_high, gen_low, gen_norm, acc, total, from_hi, from_z,
+    gen, gen_both, gen_norm, acc, total, from_hi, from_z,
     sib_send, sib_recv, far_send, far_recv, fwd_send, fwd_recv,
     z_send, z_recv, hi_send, hi_recv, red_hi_send, red_hi_recv, red_z_send, red_z_recv,
 ):
@@ -45,9 +42,7 @@
     piece = n_real // PIECES
     total_gen = n_gen * blks * reps
     total_real = n_real * blks * reps
-    tile = PAIR * n_gen
-    near_tiles = reps // PAIR
-    n_tiles = his * near_tiles
+    tile = reps * n_gen
 
     blk, rep = lax.axis_index("blk"), lax.axis_index("rep")
     hi, lo = blk // GROUP, lax.rem(blk, GROUP)
@@ -137,9 +132,10 @@
     load_bank.wait()
 
     def gather(i, carry):
+        picked = [bank[pl.ds(rows_ref[i * 8 + k], 1), :] for k in range(8)]
         for k in range(8):
             p = i * 8 + k
-            oth[pl.ds(p, 1), :] = bank[pl.ds(rows_ref[p], 1), :]
+            oth[pl.ds(p, 1), :] = picked[k]
         return carry
 
     lax.fori_loop(0, piece // 8, gather, 0)
@@ -168,11 +164,13 @@
         norm = jnp.sum(value * value, axis=1, keepdims=True)
         oth_norm[chunk] = jnp.broadcast_to(norm, (n_real, 128)).T[0:8, :]
 
-    def prepare_gen(rows):
+    def prepare_gen(q):
+        rows = tile_rows(q)
         value = gen[rows, :]
         high, low = split(value)
-        gen_high[rows, :] = high
-        gen_low[rows, :] = low
+        start = pl.multiple_of(2 * tile * q, tile)
+        gen_both[pl.ds(start, tile), :] = high
+        gen_both[pl.ds(pl.multiple_of(start + tile, tile), tile), :] = low
         gen_norm[rows, :] = jnp.sum(value * value, axis=1, keepdims=True)
 
     def tile_rows(q):
@@ -181,8 +179,10 @@
     def add_pairs(q, chunk, scale):
         rows = tile_rows(q)
         others = pl.ds(pl.multiple_of(chunk * n_real, n_real), n_real)
+        start = pl.multiple_of(2 * tile * q, tile)
         inner = product(
-            gen_high[rows, :], gen_low[rows, :], oth_high[others, :], oth_low[others, :], ((1,), (1,))
+            gen_both[pl.ds(start, 2 * tile), :], gen_both[pl.ds(start, tile), :],
+            oth_high[others, :], oth_low[others, :], ((1,), (1,)),
         )
         dist = jnp.maximum(gen_norm[rows, :] + oth_norm[chunk, 0:1, :] - 2.0 * inner, 0.0)
         wide = jnp.exp(dist * (-1.0 / (4.0 * width)))
@@ -190,11 +190,12 @@
         weight = (2.0 * (middle * middle) + middle + 0.5 * wide) * scale
         total[rows, :] += jnp.sum(weight, axis=1, keepdims=True)
         w_high, w_low = split(weight)
+        w_both = jnp.concatenate([w_high, w_low], axis=0)
         step = 256
         for column in range(0, width, step):
             columns = pl.ds(column, step)
             acc[rows, columns] += product(
-                w_high, w_low, oth_high[others, columns], oth_low[others, columns], ((1,), (0,))
+                w_both, w_high, oth_high[others, columns], oth_low[others, columns], ((1,), (0,))
             )
 
     self_scale, cross_scale = 1.0 / total_gen, -1.0 / total_real
@@ -213,7 +214,7 @@
     prepare_other(0)
     far_gen().wait_recv()
     forward_gen().start()
-    for dz in range(1, PAIR):
+    for dz in range(1, reps):
         take_z(dz)
     sib_gen().wait_recv()
     sib_real().wait_recv()
@@ -222,26 +223,18 @@
     prepare_other(2)
 
     def first_chunks(q, carry):
-        for k in range(1, near_tiles):
-
-            @pl.when(q == k)
-            def _():
-                for dz in range(k * PAIR, (k + 1) * PAIR):
-                    take_z(dz)
-
         @pl.when(q == 1)
         def _():
             for m in range(PIECES // 2):
                 take_far(m)
 
-        @pl.when(q >= near_tiles)
+        @pl.when(q >= 1)
         def _():
-            for i in range(PAIR):
-                dh, dz = q // near_tiles, lax.rem(q, near_tiles) * PAIR + i
-                hi_copy(his - dh, dz, gen_ref).wait_recv()
+            for dz in range(reps):
+                hi_copy(his - q, dz, gen_ref).wait_recv()
 
         rows = tile_rows(q)
-        prepare_gen(rows)
+        prepare_gen(q)
         acc[rows, :] = jnp.zeros((tile, width), jnp.float32)
         total[rows, :] = jnp.zeros((tile, 1), jnp.float32)
 
@@ -252,7 +245,7 @@
         lax.fori_loop(0, 3, chunk_pairs, 0)
         return carry
 
-    lax.fori_loop(0, n_tiles, first_chunks, 0)
+    lax.fori_loop(0, his, first_chunks, 0)
 
     take_far(PIECES // 2)
     for m in range(PIECES // 2):
@@ -263,7 +256,7 @@
         add_pairs(q, 3, cross_scale)
         return carry
 
-    lax.fori_loop(0, n_tiles, third_chunk, 0)
+    lax.fori_loop(0, his, third_chunk, 0)
 
     for m in range(PIECES // 2 + 1, PIECES):
         take_far(m)
@@ -272,20 +265,19 @@
     prepare_other(4)
 
     def last_chunk(i, carry):
-        q = n_tiles - 1 - i
+        q = his - 1 - i
         add_pairs(q, 4, cross_scale)
         rows = tile_rows(q)
         acc[rows, :] = total[rows, :] * gen[rows, :] - acc[rows, :]
 
-        @pl.when(q >= near_tiles)
+        @pl.when(q >= 1)
         def _():
-            for k in reversed(range(PAIR)):
-                dh, dz = q // near_tiles, lax.rem(q, near_tiles) * PAIR + k
-                red_hi(dh, dz).start()
+            for dz in reversed(range(reps)):
+                red_hi(q, dz).start()
 
         return carry
 
-    lax.fori_loop(0, n_tiles, last_chunk, 0)
+    lax.fori_loop(0, his, last_chunk, 0)
 
     for dz in reversed(range(reps)):
         for dh in range(1, his):
@@ -333,8 +325,7 @@
                 pltpu.VMEM((n_other, width), jnp.bfloat16),
                 pltpu.VMEM((5, 8, n_real), jnp.float32),
                 pltpu.VMEM((n_rows, width), jnp.float32),
-                pltpu.VMEM((n_rows, width), jnp.bfloat16),
-                pltpu.VMEM((n_rows, width), jnp.bfloat16),
+                pltpu.VMEM((2 * n_rows, width), jnp.bfloat16),
                 pltpu.VMEM((n_rows, 1), jnp.float32),
                 pltpu.VMEM((n_rows, width), jnp.float32),
                 pltpu.VMEM((n_rows, 1), jnp.float32),

time: 91 us -> 90.6 us (level)
  no operation moved by 1% of the time
where the time goes in v3:
time: 90.6 us; the launch traced here: 90 us
  Pallas kernels  88.3 us (97%)
  local copies, waits for them, and re-layouts  1.67 us (2%)
    pallas_call x1, Pallas kernels, on_device(): pl.pallas_call(functools.partial(kernel, (blks, reps)), out_shape=jax.Sha...  88.3 us

profile of v3, /device:TPU:0, one launch (start us, length us, event | category | flops | bytes accessed | tf_op | source)
XLA Modules:
  0.0 90.0 jit_solution(6659462267894201728)
XLA Ops:
  0.0 88.3 %shard_map.37 = f32[64,1024]{1,0:T(8,128)} custom-call(s32[256]{0:T(256)} %rows_ref.1, f32[64,1024]{1,0:T(8,128)} %gen_ref.1, f32[512,1024]{1,0:T(8,128)} %bank_ref.1), custom_call_target="tpu_custom_call" | custom-call | flops 8053063680 | bytes 4194304 | tf_op jit(solution)/shard_map/pallas_call | solution.py:315
  88.4 1.7 %copy.5 = f32[64,1024]{1,0:T(8,128)} copy(f32[64,1024]{1,0:T(8,128)} %shard_map.37) | data formatting | bytes 524288

commit v4 on v3

--- a/solution.py
+++ b/solution.py
@@ -9,6 +9,7 @@
 
 MESH = pl.DeviceIdType.MESH
 GROUP = 4
+ORDER = (0, 1, 3, 2)
 PIECES = 4
 
 
@@ -42,7 +43,8 @@
     piece = n_real // PIECES
     total_gen = n_gen * blks * reps
     total_real = n_real * blks * reps
-    tile = reps * n_gen
+    assert reps == len(ORDER)
+    tile = 2 * n_gen
 
     blk, rep = lax.axis_index("blk"), lax.axis_index("rep")
     hi, lo = blk // GROUP, lax.rem(blk, GROUP)
@@ -67,7 +69,7 @@
         return pl.ds(c_gen + slot * n_gen, n_gen)
 
     def block(dh, dz):
-        return pl.ds(pl.multiple_of((dh * reps + dz) * n_gen, n_gen), n_gen)
+        return pl.ds(pl.multiple_of((dh * reps + ORDER.index(dz)) * n_gen, n_gen), n_gen)
 
     def remote(src, dst, send, recv, device):
         return pltpu.make_async_remote_copy(
@@ -145,14 +147,12 @@
     z_copy(1).start()
     for dh in range(1, his):
         hi_copy(dh, 0, gen_ref).start()
-    for dz in range(2, reps):
-        z_copy(dz).start()
+    far_real(0).start()
     sib_gen().start()
-
-    far_real(0).start()
     for m in range(1, PIECES):
         lax.fori_loop(m * piece // 8, (m + 1) * piece // 8, gather, 0)
-        far_real(m).start()
+        if m == 1:
+            far_real(m).start()
     sib_real().start()
 
     def prepare_other(chunk):
@@ -209,93 +209,120 @@
         for dh in range(1, his):
             hi_copy(dh, dz, gen.at[block(0, dz)]).start()
 
+    def work(q, first, last):
+        def chunk_pairs(chunk, carry):
+            add_pairs(q, chunk, jnp.where(chunk == 2, self_scale, cross_scale))
+            return carry
+
+        lax.fori_loop(first, last, chunk_pairs, 0)
+
+    def begin(q):
+        prepare_gen(q)
+        rows = tile_rows(q)
+        acc[rows, :] = jnp.zeros((tile, width), jnp.float32)
+        total[rows, :] = jnp.zeros((tile, 1), jnp.float32)
+
+    def finish(q):
+        rows = tile_rows(q)
+        acc[rows, :] = total[rows, :] * gen[rows, :] - acc[rows, :]
+
+    def loop(first, last, step):
+        def body(i, carry):
+            step(i)
+            return carry
+
+        lax.fori_loop(first, last, body, 0)
+
     gen[block(0, 0), :] = gen_ref[...]
     oth[gen_rows(0), :] = gen_ref[...]
     prepare_other(0)
+    z_copy(1).wait_send()
+    z_copy(3).start()
+    take_z(1)
+    sib_real().wait_recv()
+    prepare_other(1)
+
+    def stage_1(dh):
+        @pl.when(dh >= 1)
+        def _():
+            for dz in ORDER[:2]:
+                hi_copy(his - dh, dz, gen_ref).wait_recv()
+
+        begin(2 * dh)
+        work(2 * dh, 0, 2)
+
+    loop(0, his, stage_1)
+    z_copy(3).wait_send()
+    z_copy(2).start()
+    take_z(3)
+    for m in range(2):
+        far_real(m).wait_send()
+    for m in range(2, PIECES):
+        far_real(m).start()
     far_gen().wait_recv()
     forward_gen().start()
-    for dz in range(1, reps):
-        take_z(dz)
+    for m in range(2):
+        take_far(m)
     sib_gen().wait_recv()
-    sib_real().wait_recv()
-    prepare_other(1)
     forward_gen().wait_recv()
     prepare_other(2)
-
-    def first_chunks(q, carry):
-        @pl.when(q == 1)
-        def _():
-            for m in range(PIECES // 2):
-                take_far(m)
-
-        @pl.when(q >= 1)
-        def _():
-            for dz in range(reps):
-                hi_copy(his - q, dz, gen_ref).wait_recv()
-
-        rows = tile_rows(q)
-        prepare_gen(q)
-        acc[rows, :] = jnp.zeros((tile, width), jnp.float32)
-        total[rows, :] = jnp.zeros((tile, 1), jnp.float32)
-
-        def chunk_pairs(chunk, inner_carry):
-            add_pairs(q, chunk, jnp.where(chunk == 2, self_scale, cross_scale))
-            return inner_carry
-
-        lax.fori_loop(0, 3, chunk_pairs, 0)
-        return carry
-
-    lax.fori_loop(0, his, first_chunks, 0)
-
-    take_far(PIECES // 2)
-    for m in range(PIECES // 2):
+    for m in range(2):
         forward_real(m).wait_recv()
     prepare_other(3)
-
-    def third_chunk(q, carry):
-        add_pairs(q, 3, cross_scale)
-        return carry
-
-    lax.fori_loop(0, his, third_chunk, 0)
-
-    for m in range(PIECES // 2 + 1, PIECES):
+    loop(0, his, lambda dh: work(2 * dh, 2, 4))
+    take_z(2)
+    begin(1)
+    work(1, 0, 4)
+    for m in range(2, PIECES):
         take_far(m)
-    for m in range(PIECES // 2, PIECES):
+    for m in range(2, PIECES):
         forward_real(m).wait_recv()
     prepare_other(4)
 
-    def last_chunk(i, carry):
-        q = his - 1 - i
-        add_pairs(q, 4, cross_scale)
-        rows = tile_rows(q)
-        acc[rows, :] = total[rows, :] * gen[rows, :] - acc[rows, :]
-
-        @pl.when(q >= 1)
-        def _():
-            for dz in reversed(range(reps)):
-                red_hi(q, dz).start()
-
-        return carry
-
-    lax.fori_loop(0, his, last_chunk, 0)
-
-    for dz in reversed(range(reps)):
+    def stage_3(dh):
+        work(2 * dh, 4, 5)
+        finish(2 * dh)
+        red_hi(dh, 1).start()
+
+    def stage_4(dh):
+        for dz in ORDER[2:]:
+            hi_copy(his - dh, dz, gen_ref).wait_recv()
+        begin(2 * dh + 1)
+        work(2 * dh + 1, 0, 5)
+        finish(2 * dh + 1)
+
+    def stage_5(q):
+        work(q, 4, 5)
+        finish(q)
+
+    loop(1, his, stage_3)
+    loop(1, his, stage_4)
+    sends = (1, 2, 3, 0)
+    for dh in range(1, his):
+        red_hi(dh, 1).wait_send()
+        red_hi(dh, 2).start()
+    loop(0, 2, stage_5)
+
+    for i, dz in enumerate(sends):
         for dh in range(1, his):
             red_hi(his - dh, dz).wait_recv()
             acc[block(0, dz), :] += from_hi[dh, dz]
         if dz > 0:
             red_z(dz).start()
+        if i + 2 < len(sends):
+            for dh in range(1, his):
+                red_hi(dh, sends[i + 1]).wait_send()
+                red_hi(dh, sends[i + 2]).start()
     result = acc[block(0, 0), :]
-    for dz in reversed(range(1, reps)):
+    for dz in sends[:-1]:
         red_z(reps - dz).wait_recv()
         result = result + from_z[dz]
     out_ref[...] = result
 
-    sent = [far_gen(), sib_gen(), sib_real(), forward_gen()]
-    sent += [far_real(m) for m in range(PIECES)] + [forward_real(m) for m in range(PIECES)]
-    sent += [z_copy(dz) for dz in range(1, reps)] + [red_z(dz) for dz in range(1, reps)]
+    sent = [far_gen(), sib_gen(), sib_real(), forward_gen(), z_copy(2)]
+    sent += [far_real(m) for m in range(2, PIECES)] + [forward_real(m) for m in range(PIECES)]
     sent += [hi_copy(dh, dz, gen_ref) for dh in range(1, his) for dz in range(reps)]
-    sent += [red_hi(dh, dz) for dh in range(1, his) for dz in range(reps)]
+    sent += [red_hi(dh, 0) for dh in range(1, his)] + [red_z(dz) for dz in range(1, reps)]
     for copy in sent:
         copy.wait_send()
 

time: 90.6 us -> 84.3 us (0.930)
  the two profiles are of different devices: /device:TPU:0 before, /device:TPU:11 now
where the time goes in v4:
time: 84.3 us; the launch traced here: 84.1 us
  Pallas kernels  82.4 us (98%)
  local copies, waits for them, and re-layouts  1.67 us (2%)
    pallas_call x1, Pallas kernels, on_device(): pl.pallas_call(functools.partial(kernel, (blks, reps)), out_shape=jax.Sha...  82.4 us

profile of v4, /device:TPU:11, one launch (start us, length us, event | category | flops | bytes accessed | tf_op | source)
XLA Modules:
  0.0 84.1 jit_solution(9233165790125258936)
XLA Ops:
  0.0 82.4 %shard_map.37 = f32[64,1024]{1,0:T(8,128)} custom-call(s32[256]{0:T(256)} %rows_ref.1, f32[64,1024]{1,0:T(8,128)} %gen_ref.1, f32[512,1024]{1,0:T(8,128)} %bank_ref.1), custom_call_target="tpu_custom_call" | custom-call | flops 8053063680 | bytes 4194304 | tf_op jit(solution)/shard_map/pallas_call | solution.py:342
  82.4 1.7 %copy.5 = f32[64,1024]{1,0:T(8,128)} copy(f32[64,1024]{1,0:T(8,128)} %shard_map.37) | data formatting | bytes 524288

commit v5 on v4

--- a/solution.py
+++ b/solution.py
@@ -10,6 +10,7 @@
 MESH = pl.DeviceIdType.MESH
 GROUP = 4
 ORDER = (0, 1, 3, 2)
+PARTS = 2
 PIECES = 4
 
 
@@ -110,17 +111,24 @@
             fwd_send.at[1 + m], fwd_recv.at[1 + m], sibling,
         )
 
-    def red_hi(dh, dz):
+    n_part = n_gen // PARTS
+
+    def part_of(dh, dz, p):
+        start = (dh * reps + ORDER.index(dz)) * n_gen + p * n_part
+        return pl.ds(pl.multiple_of(start, n_part), n_part)
+
+    def red_hi(dh, dz, p):
         back = his - dh
         return remote(
-            acc.at[block(dh, dz)], from_hi.at[back, dz],
-            red_hi_send.at[dh, dz], red_hi_recv.at[back, dz], hi_partner(dh),
-        )
-
-    def red_z(dz):
+            acc.at[part_of(dh, dz, p)], from_hi.at[back, dz, pl.ds(p * n_part, n_part)],
+            red_hi_send.at[dh, dz, p], red_hi_recv.at[back, dz, p], hi_partner(dh),
+        )
+
+    def red_z(dz, p):
         back = reps - dz
         return remote(
-            acc.at[block(0, dz)], from_z.at[back], red_z_send.at[dz], red_z_recv.at[back], z_partner(dz)
+            acc.at[part_of(0, dz, p)], from_z.at[back, pl.ds(p * n_part, n_part)],
+            red_z_send.at[dz, p], red_z_recv.at[back, p], z_partner(dz),
         )
 
     load_bank = pltpu.make_async_copy(bank_ref, bank, bank_sem)
@@ -155,14 +163,18 @@
             far_real(m).start()
     sib_real().start()
 
-    def prepare_other(chunk):
-        rows = pl.ds(chunk * n_real, n_real)
+    def prepare_half(chunk, which):
+        rows = pl.ds(chunk * n_real + which * half, half)
         value = oth[rows, :]
         high, low = split(value)
         oth_high[rows, :] = high
         oth_low[rows, :] = low
         norm = jnp.sum(value * value, axis=1, keepdims=True)
-        oth_norm[chunk] = jnp.broadcast_to(norm, (n_real, 128)).T[0:8, :]
+        oth_norm[chunk, :, which * half : (which + 1) * half] = jnp.broadcast_to(norm, (half, 128)).T[0:8, :]
+
+    def prepare_other(chunk):
+        prepare_half(chunk, 0)
+        prepare_half(chunk, 1)
 
     def prepare_gen(q):
         rows = tile_rows(q)
@@ -239,6 +251,7 @@
     z_copy(1).wait_send()
     z_copy(3).start()
     take_z(1)
+    far_real(2).start()
     sib_real().wait_recv()
     prepare_other(1)
 
@@ -255,10 +268,7 @@
     z_copy(3).wait_send()
     z_copy(2).start()
     take_z(3)
-    for m in range(2):
-        far_real(m).wait_send()
-    for m in range(2, PIECES):
-        far_real(m).start()
+    far_real(3).start()
     far_gen().wait_recv()
     forward_gen().start()
     for m in range(2):
@@ -275,14 +285,16 @@
     work(1, 0, 4)
     for m in range(2, PIECES):
         take_far(m)
+    prepare_half(4, 0)
     for m in range(2, PIECES):
         forward_real(m).wait_recv()
-    prepare_other(4)
+    prepare_half(4, 1)
 
     def stage_3(dh):
         work(2 * dh, 4, 5)
         finish(2 * dh)
-        red_hi(dh, 1).start()
+        for p in range(PARTS):
+            red_hi(dh, 1, p).start()
 
     def stage_4(dh):
         for dz in ORDER[2:]:
@@ -297,32 +309,40 @@
 
     loop(1, his, stage_3)
     loop(1, his, stage_4)
-    sends = (1, 2, 3, 0)
-    for dh in range(1, his):
-        red_hi(dh, 1).wait_send()
-        red_hi(dh, 2).start()
+    sends = [(dz, p) for dz in (1, 2, 3, 0) for p in range(PARTS)]
+
+    def next_send(i):
+        for dh in range(1, his):
+            red_hi(dh, *sends[i]).wait_send()
+            red_hi(dh, *sends[i + 2]).start()
+
+    next_send(0)
+    next_send(1)
     loop(0, 2, stage_5)
 
-    for i, dz in enumerate(sends):
+    for i, (dz, p) in enumerate(sends):
+        rows = part_of(0, dz, p)
+        value = acc[rows, :]
         for dh in range(1, his):
-            red_hi(his - dh, dz).wait_recv()
-            acc[block(0, dz), :] += from_hi[dh, dz]
+            red_hi(his - dh, dz, p).wait_recv()
+            value = value + from_hi[dh, dz, pl.ds(p * n_part, n_part), :]
+        acc[rows, :] = value
         if dz > 0:
-            red_z(dz).start()
-        if i + 2 < len(sends):
-            for dh in range(1, his):
-                red_hi(dh, sends[i + 1]).wait_send()
-                red_hi(dh, sends[i + 2]).start()
-    result = acc[block(0, 0), :]
-    for dz in sends[:-1]:
-        red_z(reps - dz).wait_recv()
-        result = result + from_z[dz]
-    out_ref[...] = result
+            red_z(dz, p).start()
+        if i + 4 < len(sends):
+            next_send(i + 2)
+    for p in range(PARTS):
+        result = acc[part_of(0, 0, p), :]
+        for dz in (1, 2, 3):
+            red_z(reps - dz, p).wait_recv()
+            result = result + from_z[dz, pl.ds(p * n_part, n_part), :]
+        out_ref[pl.ds(p * n_part, n_part), :] = result
 
     sent = [far_gen(), sib_gen(), sib_real(), forward_gen(), z_copy(2)]
-    sent += [far_real(m) for m in range(2, PIECES)] + [forward_real(m) for m in range(PIECES)]
+    sent += [far_real(m) for m in range(PIECES)] + [forward_real(m) for m in range(PIECES)]
     sent += [hi_copy(dh, dz, gen_ref) for dh in range(1, his) for dz in range(reps)]
-    sent += [red_hi(dh, 0) for dh in range(1, his)] + [red_z(dz) for dz in range(1, reps)]
+    sent += [red_hi(dh, 0, p) for dh in range(1, his) for p in range(PARTS)]
+    sent += [red_z(dz, p) for dz in range(1, reps) for p in range(PARTS)]
     for copy in sent:
         copy.wait_send()
 
@@ -363,8 +383,8 @@
                 dma((1 + PIECES,)), dma((1 + PIECES,)),
                 dma((reps,)), dma((reps,)),
                 dma((his, reps)), dma((his, reps)),
-                dma((his, reps)), dma((his, reps)),
-                dma((reps,)), dma((reps,)),
+                dma((his, reps, PARTS)), dma((his, reps, PARTS)),
+                dma((reps, PARTS)), dma((reps, PARTS)),
             ],
             compiler_params=pltpu.CompilerParams(
                 collective_id=0, has_side_effects=True, vmem_limit_bytes=60 * 1024 * 1024

time: 84.3 us -> 82.5 us (0.979)
  the two profiles are of different devices: /device:TPU:11 before, /device:TPU:13 now
where the time goes in v5:
time: 82.5 us; the launch traced here: 82.3 us
  Pallas kernels  80.6 us (98%)
  local copies, waits for them, and re-layouts  1.67 us (2%)
    pallas_call x1, Pallas kernels, on_device(): pl.pallas_call(functools.partial(kernel, (blks, reps)), out_shape=jax.Sha...  80.6 us
    unnamed x1, local copies, waits for them, and re-layouts  1.67 us

profile of v5, /device:TPU:13, one launch (start us, length us, event | category | flops | bytes accessed | tf_op | source)
XLA Modules:
  0.0 82.3 jit_solution(16364050664411525747)
XLA Ops:
  0.0 80.6 %shard_map.37 = f32[64,1024]{1,0:T(8,128)} custom-call(s32[256]{0:T(256)} %rows_ref.1, f32[64,1024]{1,0:T(8,128)} %gen_ref.1, f32[512,1024]{1,0:T(8,128)} %bank_ref.1), custom_call_target="tpu_custom_call" | custom-call | flops 8053063680 | bytes 4194304 | tf_op jit(solution)/shard_map/pallas_call | solution.py:362
  80.6 1.7 %copy.5 = f32[64,1024]{1,0:T(8,128)} copy(f32[64,1024]{1,0:T(8,128)} %shard_map.37) | data formatting | bytes 524288

commit v6 on v5

--- a/solution.py
+++ b/solution.py
@@ -31,7 +31,7 @@
 
 def kernel(
     sizes,
-    rows_ref, gen_ref, bank_ref, out_ref, bank, bank_sem,
+    gen_ref, real_ref, out_ref,
     oth, oth_high, oth_low, oth_norm,
     gen, gen_both, gen_norm, acc, total, from_hi, from_z,
     sib_send, sib_recv, far_send, far_recv, fwd_send, fwd_recv,
@@ -40,7 +40,7 @@
     blks, reps = sizes
     his = blks // GROUP
     n_gen, width = gen_ref.shape
-    n_real = rows_ref.shape[0]
+    n_real = real_ref.shape[0]
     piece = n_real // PIECES
     total_gen = n_gen * blks * reps
     total_real = n_real * blks * reps
@@ -90,7 +90,7 @@
 
     def far_real(m):
         return remote(
-            oth.at[pl.ds(m * piece, piece)], oth.at[far_rows(m, False)],
+            real_ref.at[pl.ds(m * piece, piece)], oth.at[far_rows(m, False)],
             far_send.at[1 + m], far_recv.at[1 + m], across,
         )
 
@@ -99,7 +99,7 @@
 
     def sib_real():
         return remote(
-            oth.at[pl.ds(0, n_real)], oth.at[pl.ds(n_real, n_real)], sib_send.at[1], sib_recv.at[1], sibling
+            real_ref, oth.at[pl.ds(n_real, n_real)], sib_send.at[1], sib_recv.at[1], sibling
         )
 
     def forward_gen():
@@ -131,24 +131,12 @@
             red_z_send.at[dz, p], red_z_recv.at[back, p], z_partner(dz),
         )
 
-    load_bank = pltpu.make_async_copy(bank_ref, bank, bank_sem)
-    load_bank.start()
     partners = [sibling, across]
     partners += [z_partner(dz) for dz in range(1, reps)]
     partners += [hi_partner(dh) for dh in range(1, his)]
     barrier = pltpu.get_barrier_semaphore()
     for device in partners:
         pl.semaphore_signal(barrier, inc=1, device_id=device, device_id_type=MESH)
-    load_bank.wait()
-
-    def gather(i, carry):
-        picked = [bank[pl.ds(rows_ref[i * 8 + k], 1), :] for k in range(8)]
-        for k in range(8):
-            p = i * 8 + k
-            oth[pl.ds(p, 1), :] = picked[k]
-        return carry
-
-    lax.fori_loop(0, piece // 8, gather, 0)
     pl.semaphore_wait(barrier, len(partners))
 
     far_gen().start()
@@ -157,15 +145,12 @@
         hi_copy(dh, 0, gen_ref).start()
     far_real(0).start()
     sib_gen().start()
-    for m in range(1, PIECES):
-        lax.fori_loop(m * piece // 8, (m + 1) * piece // 8, gather, 0)
-        if m == 1:
-            far_real(m).start()
+    far_real(1).start()
     sib_real().start()
 
     def prepare_half(chunk, which):
         rows = pl.ds(chunk * n_real + which * half, half)
-        value = oth[rows, :]
+        value = real_ref[rows, :] if chunk == 0 else oth[rows, :]
         high, low = split(value)
         oth_high[rows, :] = high
         oth_low[rows, :] = low
@@ -362,11 +347,9 @@
         return pl.pallas_call(
             functools.partial(kernel, (blks, reps)),
             out_shape=jax.ShapeDtypeStruct((n_gen, width), jnp.float32),
-            in_specs=[pl.BlockSpec(memory_space=pltpu.SMEM), vmem, pl.BlockSpec(memory_space=pl.ANY)],
+            in_specs=[vmem, vmem],
             out_specs=vmem,
             scratch_shapes=[
-                pltpu.VMEM(real_bank.shape, jnp.float32),
-                dma(()),
                 pltpu.VMEM((n_other, width), jnp.float32),
                 pltpu.VMEM((n_other, width), jnp.bfloat16),
                 pltpu.VMEM((n_other, width), jnp.bfloat16),
@@ -392,7 +375,7 @@
             cost_estimate=pl.CostEstimate(
                 flops=12 * pairs * width, bytes_accessed=4 * 1024 * width, transcendentals=pairs
             ),
-        )(subset_rows, generated, real_bank)
+        )(generated, real_bank.at[subset_rows].get(mode="promise_in_bounds", wrap_negative_indices=False))
 
     in_specs = (P(("blk", "rep"), None), P(("blk", "rep"), None), P(("blk", "rep")))
     return jax.shard_map(

time: 82.5 us -> 85.2 us (1.033)
  the two profiles are of different devices: /device:TPU:13 before, /device:TPU:9 now
where the time goes in v6:
time: 85.2 us; the launch traced here: 85 us
  Pallas kernels  79.7 us (94%)
  local copies, waits for them, and re-layouts  4.48 us (5%)
    pallas_call x1, Pallas kernels, on_device(): pl.pallas_call(functools.partial(kernel, (blks, reps)), out_shape=jax.Sha...  79.7 us
    unnamed x3, local copies, waits for them, and re-layouts  2.45 us
    gather x1, local copies, waits for them, and re-layouts, on_device(): real_bank.at[subset_rows]  2.03 us

profile of v6, /device:TPU:9, one launch (start us, length us, event | category | flops | bytes accessed | tf_op | source)
XLA Modules:
  0.0 85.0 jit_solution(3773624342301495288)
XLA Ops:
  0.0 0.0 copy-start
  0.0 0.8 pad_clamp_fusion
  0.8 0.8 copy-done
  1.6 2.0 %gather_fusion = f32[256,1024]{1,0:T(8,128)} fusion(f32[512,1024]{1,0:T(8,128)S(1)} %copy-done, s32[1024]{0:T(1024)S(1)} %pad_clamp_fusion), kind=kCustom, calls=%fused_computation | custom fusion | bytes 2098176 | tf_op jit(solution)/shard_map/gather | solution.py:378
  3.6 79.7 %shard_map.37 = f32[64,1024]{1,0:T(8,128)} custom-call(f32[64,1024]{1,0:T(8,128)} %gen_ref.1, f32[256,1024]{1,0:T(8,128)} %gather_fusion), custom_call_target="tpu_custom_call" | custom-call | flops 8053063680 | bytes 4194304 | tf_op jit(solution)/shard_map/pallas_call | solution.py:347
  83.3 1.7 %copy.5 = f32[64,1024]{1,0:T(8,128)} copy(f32[64,1024]{1,0:T(8,128)} %shard_map.37) | data formatting | bytes 524288
Async XLA Ops:
  0.0 1.6 %copy-start = (f32[512,1024]{1,0:T(8,128)S(1)}, f32[512,1024]{1,0:T(8,128)}, u32[]{:S(2)}) copy-start(f32[512,1024]{1,0:T(8,128)} %param.4) | copy-start | bytes 6291460

commit v7 on v5

--- a/solution.py
+++ b/solution.py
@@ -31,7 +31,7 @@
 
 def kernel(
     sizes,
-    rows_ref, gen_ref, bank_ref, out_ref, bank, bank_sem,
+    rows_ref, gen_ref, bank_ref, out_ref, bank, load_sem,
     oth, oth_high, oth_low, oth_norm,
     gen, gen_both, gen_norm, acc, total, from_hi, from_z,
     sib_send, sib_recv, far_send, far_recv, fwd_send, fwd_recv,
@@ -72,6 +72,8 @@
     def block(dh, dz):
         return pl.ds(pl.multiple_of((dh * reps + ORDER.index(dz)) * n_gen, n_gen), n_gen)
 
+    own = gen.at[block(0, 0)]
+
     def remote(src, dst, send, recv, device):
         return pltpu.make_async_remote_copy(
             src_ref=src, dst_ref=dst, send_sem=send, recv_sem=recv, device_id=device, device_id_type=MESH
@@ -79,14 +81,14 @@
 
     def z_copy(dz):
         back = reps - dz
-        return remote(gen_ref, gen.at[block(0, back)], z_send.at[dz], z_recv.at[back], z_partner(dz))
+        return remote(own, gen.at[block(0, back)], z_send.at[dz], z_recv.at[back], z_partner(dz))
 
     def hi_copy(dh, dz, src):
         back = his - dh
         return remote(src, gen.at[block(back, dz)], hi_send.at[dh, dz], hi_recv.at[back, dz], hi_partner(dh))
 
     def far_gen():
-        return remote(gen_ref, oth.at[gen_rows(2)], far_send.at[0], far_recv.at[0], across)
+        return remote(own, oth.at[gen_rows(2)], far_send.at[0], far_recv.at[0], across)
 
     def far_real(m):
         return remote(
@@ -95,7 +97,7 @@
         )
 
     def sib_gen():
-        return remote(gen_ref, oth.at[gen_rows(1)], sib_send.at[0], sib_recv.at[0], sibling)
+        return remote(own, oth.at[gen_rows(1)], sib_send.at[0], sib_recv.at[0], sibling)
 
     def sib_real():
         return remote(
@@ -131,15 +133,21 @@
             red_z_send.at[dz, p], red_z_recv.at[back, p], z_partner(dz),
         )
 
-    load_bank = pltpu.make_async_copy(bank_ref, bank, bank_sem)
-    load_bank.start()
+    loads = [
+        pltpu.make_async_copy(bank_ref, bank, load_sem.at[0]),
+        pltpu.make_async_copy(gen_ref, own, load_sem.at[1]),
+        pltpu.make_async_copy(gen_ref, oth.at[gen_rows(0)], load_sem.at[2]),
+    ]
+    for load in loads:
+        load.start()
     partners = [sibling, across]
     partners += [z_partner(dz) for dz in range(1, reps)]
     partners += [hi_partner(dh) for dh in range(1, his)]
     barrier = pltpu.get_barrier_semaphore()
     for device in partners:
         pl.semaphore_signal(barrier, inc=1, device_id=device, device_id_type=MESH)
-    load_bank.wait()
+    for load in loads:
+        load.wait()
 
     def gather(i, carry):
         picked = [bank[pl.ds(rows_ref[i * 8 + k], 1), :] for k in range(8)]
@@ -154,7 +162,7 @@
     far_gen().start()
     z_copy(1).start()
     for dh in range(1, his):
-        hi_copy(dh, 0, gen_ref).start()
+        hi_copy(dh, 0, own).start()
     far_real(0).start()
     sib_gen().start()
     for m in range(1, PIECES):
@@ -245,11 +253,10 @@
 
         lax.fori_loop(first, last, body, 0)
 
-    gen[block(0, 0), :] = gen_ref[...]
-    oth[gen_rows(0), :] = gen_ref[...]
     prepare_other(0)
     z_copy(1).wait_send()
     z_copy(3).start()
+    z_copy(2).start()
     take_z(1)
     far_real(2).start()
     sib_real().wait_recv()
@@ -259,14 +266,12 @@
         @pl.when(dh >= 1)
         def _():
             for dz in ORDER[:2]:
-                hi_copy(his - dh, dz, gen_ref).wait_recv()
+                hi_copy(his - dh, dz, own).wait_recv()
 
         begin(2 * dh)
         work(2 * dh, 0, 2)
 
     loop(0, his, stage_1)
-    z_copy(3).wait_send()
-    z_copy(2).start()
     take_z(3)
     far_real(3).start()
     far_gen().wait_recv()
@@ -279,8 +284,8 @@
     for m in range(2):
         forward_real(m).wait_recv()
     prepare_other(3)
+    take_z(2)
     loop(0, his, lambda dh: work(2 * dh, 2, 4))
-    take_z(2)
     begin(1)
     work(1, 0, 4)
     for m in range(2, PIECES):
@@ -298,7 +303,7 @@
 
     def stage_4(dh):
         for dz in ORDER[2:]:
-            hi_copy(his - dh, dz, gen_ref).wait_recv()
+            hi_copy(his - dh, dz, own).wait_recv()
         begin(2 * dh + 1)
         work(2 * dh + 1, 0, 5)
         finish(2 * dh + 1)
@@ -338,9 +343,9 @@
             result = result + from_z[dz, pl.ds(p * n_part, n_part), :]
         out_ref[pl.ds(p * n_part, n_part), :] = result
 
-    sent = [far_gen(), sib_gen(), sib_real(), forward_gen(), z_copy(2)]
+    sent = [far_gen(), sib_gen(), sib_real(), forward_gen(), z_copy(2), z_copy(3)]
     sent += [far_real(m) for m in range(PIECES)] + [forward_real(m) for m in range(PIECES)]
-    sent += [hi_copy(dh, dz, gen_ref) for dh in range(1, his) for dz in range(reps)]
+    sent += [hi_copy(dh, dz, own) for dh in range(1, his) for dz in range(reps)]
     sent += [red_hi(dh, 0, p) for dh in range(1, his) for p in range(PARTS)]
     sent += [red_z(dz, p) for dz in range(1, reps) for p in range(PARTS)]
     for copy in sent:
@@ -362,11 +367,11 @@
         return pl.pallas_call(
             functools.partial(kernel, (blks, reps)),
             out_shape=jax.ShapeDtypeStruct((n_gen, width), jnp.float32),
-            in_specs=[pl.BlockSpec(memory_space=pltpu.SMEM), vmem, pl.BlockSpec(memory_space=pl.ANY)],
+            in_specs=[pl.BlockSpec(memory_space=pltpu.SMEM)] + [pl.BlockSpec(memory_space=pl.ANY)] * 2,
             out_specs=vmem,
             scratch_shapes=[
                 pltpu.VMEM(real_bank.shape, jnp.float32),
-                dma(()),
+                dma((3,)),
                 pltpu.VMEM((n_other, width), jnp.float32),
                 pltpu.VMEM((n_other, width), jnp.bfloat16),
                 pltpu.VMEM((n_other, width), jnp.bfloat16),

time: 82.5 us -> 81.9 us (level)
  the two profiles are of different devices: /device:TPU:13 before, /device:TPU:24 now
where the time goes in v7:
time: 81.9 us; the launch traced here: 81.7 us
  Pallas kernels  80 us (98%)
  local copies, waits for them, and re-layouts  1.67 us (2%)
    pallas_call x1, Pallas kernels, on_device(): pl.pallas_call(functools.partial(kernel, (blks, reps)), out_shape=jax.Sha...  80 us
    unnamed x1, local copies, waits for them, and re-layouts  1.67 us

profile of v7, /device:TPU:24, one launch (start us, length us, event | category | flops | bytes accessed | tf_op | source)
XLA Modules:
  0.0 81.7 jit_solution(15104678492240694835)
XLA Ops:
  0.0 80.0 %shard_map.37 = f32[64,1024]{1,0:T(8,128)} custom-call(s32[256]{0:T(256)} %rows_ref.1, f32[64,1024]{1,0:T(8,128)} %gen_ref.1, f32[512,1024]{1,0:T(8,128)} %bank_ref.1), custom_call_target="tpu_custom_call" | custom-call | flops 8053063680 | bytes 4194304 | tf_op jit(solution)/shard_map/pallas_call | solution.py:367
  80.0 1.7 %copy.5 = f32[64,1024]{1,0:T(8,128)} copy(f32[64,1024]{1,0:T(8,128)} %shard_map.37) | data formatting | bytes 524288

commit v8 on v7

--- a/solution.py
+++ b/solution.py
@@ -287,9 +287,10 @@
     take_z(2)
     loop(0, his, lambda dh: work(2 * dh, 2, 4))
     begin(1)
-    work(1, 0, 4)
-    for m in range(2, PIECES):
-        take_far(m)
+    work(1, 0, 2)
+    take_far(2)
+    work(1, 2, 4)
+    take_far(3)
     prepare_half(4, 0)
     for m in range(2, PIECES):
         forward_real(m).wait_recv()

time: 81.9 us -> 81.9 us (level)
  no operation moved by 1% of the time
where the time goes in v8:
time: 81.9 us; the launch traced here: 81.7 us
  Pallas kernels  80 us (98%)
  local copies, waits for them, and re-layouts  1.67 us (2%)
    pallas_call x1, Pallas kernels, on_device(): pl.pallas_call(functools.partial(kernel, (blks, reps)), out_shape=jax.Sha...  80 us
    unnamed x1, local copies, waits for them, and re-layouts  1.67 us

profile of v8, /device:TPU:24, one launch (start us, length us, event | category | flops | bytes accessed | tf_op | source)
XLA Modules:
  0.0 81.7 jit_solution(2287649058891040797)
XLA Ops:
  0.0 80.0 %shard_map.37 = f32[64,1024]{1,0:T(8,128)} custom-call(s32[256]{0:T(256)} %rows_ref.1, f32[64,1024]{1,0:T(8,128)} %gen_ref.1, f32[512,1024]{1,0:T(8,128)} %bank_ref.1), custom_call_target="tpu_custom_call" | custom-call | flops 8053063680 | bytes 4194304 | tf_op jit(solution)/shard_map/pallas_call | solution.py:368
  80.0 1.7 %copy.5 = f32[64,1024]{1,0:T(8,128)} copy(f32[64,1024]{1,0:T(8,128)} %shard_map.37) | data formatting | bytes 524288
